TPU v7x, 32 devices: a whole 2x2x4 slice. The times are simulated.
32 devices in a mesh: grp: 2 (over x), ch: 16 (over z, y, core).
Axes of the slice: x: 2, y: 2, z: 4, core: 2. Of those that a mesh axis runs over, the one named last changes fastest.
Arguments:
- features: bfloat16 [2048, 2048], P('ch', 'grp'), parts along dimension 1, may hold values from -50 to 50
- dw_weight: float32 [2048, 49], P('ch'), may hold values from -0.875 to 0.875
- norm_gain: float32 [2048], replicated, may hold values from 0.25 to 1.75
- layer_scale: float32 [2048], replicated, may hold values from 0.2 to 1
- w_in: bfloat16 [8192, 2048], P('ch'), may hold values from -0.125 to 0.125
- w_out: bfloat16 [8192, 2048], P('ch'), may hold values from -0.0625 to 0.0625
- w_head: bfloat16 [2048, 150], replicated, may hold values from -3 to 3
- labels: int32 [2048], P('grp'), parts along dimension 0, may hold values from 0 to 149
Outputs:
- d_features: float32 [2048, 2048], P('ch', 'grp'), parts along dimension 1
- d_dw: float32 [2048, 98], P('ch', 'grp'), parts along dimension 1
- d_scale: float32 [4096], P(('grp', 'ch')), parts along dimension 0
- d_w_in: float32 [16384, 2048], P(('grp', 'ch')), parts along dimension 0
- d_w_out: float32 [16384, 2048], P(('grp', 'ch')), parts along dimension 0
- d_head: float32 [2048, 300], P('ch', 'grp'), parts along dimension 1
- mean_loss: float32 [2], P('grp'), parts along dimension 0
There are 2 independent parts, one for each index of `grp`. A program takes and returns all parts, laid end to end along the dimension named above; an argument that names none is the same for every part. Nothing has to cross between parts.
All inputs are finite; a program needn't handle non-finite values.
Results may differ from a plain program's by a relative error of at most 0.012.
Values may be sent and summed in bfloat16 or wider, within the bound.
A program may use at most 128 MiB of HBM per device.

v0:
```python
import jax
import jax.numpy as jnp
from jax import lax
from jax.sharding import PartitionSpec as P

KS = 7
WIN_H = 32
WIN_W = 32
norm_eps = 1e-06


def conv_apply(in_grid, kernel):
    half = KS // 2
    padded = jnp.pad(in_grid, ((0, 0), (half, half), (half, half)))
    running = jnp.zeros(in_grid.shape, in_grid.dtype)
    for row_shift in range(KS):
        for col_shift in range(KS):
            tap = kernel[:, row_shift * KS + col_shift]
            running = (
                running
                + tap[:, None, None]
                * padded[:, row_shift : row_shift + WIN_H, col_shift : col_shift + WIN_W]
            )
    return running


def gelu_parts(values):
    cum_prob = 0.5 * (1.0 + lax.erf(values * 0.7071067811865476))
    density = jnp.exp(-0.5 * values * values) * 0.3989422804014327
    return (values * cum_prob, cum_prob + values * density)


def per_device(features, dw_weight, norm_gain, layer_scale, w_in, w_out, w_head, labels):
    highest = lax.Precision.HIGHEST
    my_rows = features.shape[0]
    tok_count = features.shape[1]
    class_count = w_head.shape[1]
    row_offset = lax.axis_index("ch") * my_rows
    inputs_wide = features.astype(jnp.float32)
    in_grid = inputs_wide.reshape(my_rows, WIN_H, WIN_W)
    conv_out = conv_apply(in_grid, dw_weight).reshape(my_rows, tok_count).astype(jnp.bfloat16)
    conv_all = lax.all_gather(conv_out, "ch", axis=0, tiled=True)
    conv_wide = conv_all.astype(jnp.float32)
    tok_mean = jnp.mean(conv_wide, axis=0)
    centered = conv_wide - tok_mean[None, :]
    tok_var = jnp.mean(centered * centered, axis=0)
    inv_std = 1.0 / jnp.sqrt(tok_var + norm_eps)
    normed = centered * inv_std[None, :]
    norm_out = (norm_gain[:, None] * normed).astype(jnp.bfloat16)
    pre_act = jnp.dot(w_in, norm_out, preferred_element_type=jnp.float32)
    gelu_out, gelu_slope = gelu_parts(pre_act)
    hidden = gelu_out.astype(jnp.bfloat16)
    my_scale = lax.dynamic_slice_in_dim(layer_scale, row_offset, my_rows, 0)
    head_wide = w_head.astype(jnp.float32)
    my_head = lax.dynamic_slice_in_dim(head_wide, row_offset, my_rows, 0)
    w_cols = w_out
    branch_sum = lax.psum_scatter(
        lax.dot_general(
            w_cols, hidden, (((0,), (0,)), ((), ())), preferred_element_type=jnp.float32
        ),
        "ch",
        scatter_dimension=0,
        tiled=True,
    )
    block_out = inputs_wide + my_scale[:, None] * branch_sum
    part_logits = lax.dot_general(block_out, my_head, (((0,), (0,)), ((), ())), precision=highest)
    logits = lax.psum(part_logits, "ch")
    row_max = jnp.max(logits, axis=1, keepdims=True)
    exp_terms = jnp.exp(logits - row_max)
    exp_total = jnp.sum(exp_terms, axis=1, keepdims=True)
    log_total = jnp.log(exp_total) + row_max
    onehot = (labels[:, None] == jnp.arange(class_count, dtype=jnp.int32)[None, :]).astype(
        jnp.float32
    )
    picked = jnp.sum(logits * onehot, axis=1)
    mean_loss = jnp.mean(log_total[:, 0] - picked).reshape(1)
    logit_grad = exp_terms / exp_total - onehot
    out_grad = lax.dot_general(my_head, logit_grad, (((1,), (1,)), ((), ())), precision=highest)
    d_head = jnp.dot(block_out, logit_grad, precision=highest)
    d_scale = jnp.sum(out_grad * branch_sum, axis=1)
    branch_grad = (my_scale[:, None] * out_grad).astype(jnp.bfloat16)
    incoming = lax.all_gather(branch_grad, "ch", axis=0, tiled=True)
    w_cols = w_out
    hidden_acc = jnp.dot(w_cols, incoming, preferred_element_type=jnp.float32)
    tile_grad = lax.dot_general(
        hidden, incoming, (((1,), (1,)), ((), ())), preferred_element_type=jnp.float32
    )
    pre_grad = (hidden_acc * gelu_slope).astype(jnp.bfloat16)
    d_w_in = lax.dot_general(
        pre_grad, norm_out, (((1,), (1,)), ((), ())), preferred_element_type=jnp.float32
    )
    norm_grad = lax.dot_general(
        w_in, pre_grad, (((0,), (0,)), ((), ())), preferred_element_type=jnp.float32
    )
    gained = norm_gain[:, None] * norm_grad
    conv_term = (
        gained
        - jnp.mean(gained, axis=0)[None, :]
        - normed * jnp.mean(gained * normed, axis=0)[None, :]
    ) * inv_std[None, :]
    conv_grad = lax.psum_scatter(conv_term, "ch", scatter_dimension=0, tiled=True)
    unused, pullback = jax.vjp(conv_apply, in_grid, dw_weight)
    grid_grad, d_dw = pullback(conv_grad.reshape(my_rows, WIN_H, WIN_W))
    d_features = out_grad + grid_grad.reshape(my_rows, tok_count)
    return (d_features, d_dw, d_scale, d_w_in, tile_grad, d_head, mean_loss)


def solution(mesh):
    placed = (P("ch", "grp"), P("ch", None), P(), P(), P("ch", None), P("ch", None), P(), P("grp"))
    return jax.shard_map(
        per_device,
        mesh=mesh,
        in_specs=placed,
        out_specs=(
            P("ch", "grp"),
            P("ch", "grp"),
            P(("grp", "ch")),
            P(("grp", "ch"), None),
            P(("grp", "ch"), None),
            P("ch", "grp"),
            P("grp"),
        ),
        check_vma=False,
    )
```

profile of v0, /device:TPU:0, one launch (start us, length us, event | category | flops | bytes accessed | tf_op | source)
XLA Modules:
  0.0 497.7 jit_solution(14007070145774544614)
XLA Ops:
  10.4 1.1 copy.19
  11.6 4.8 add_convert_fusion
  16.5 56.0 %all-gather.3.cloned.1.call-done = bf16[2048,1024]{0,1:T(8,128)(2,1)} async-done(((bf16[128,1024]{0,1:T(8,128)(2,1)}), bf16[2048,1024]{0,1:T(8,128)(2,1)}) %all-gather.3.cloned.1.call-update) | async-done | bytes 4194320 | tf_op jit(solution)/shard_map/all_gather | solution.py:42
  72.5 3.0 convert_reduce_fusion
  75.9 1.2 fusion.9
  77.3 1.6 fusion.5
  79.0 2.4 fusion.31
  81.4 1.3 copy-done.7
  82.7 5.6 %convolution_bitcast_fusion = f32[2048,1024]{0,1:T(8,128)} fusion(bf16[512,2048]{1,0:T(8,128)(2,1)S(1)} %copy-done.45, f32[1024,512]{1,0:T(8,128)S(1)} %fusion.31), kind=kOutput, calls=%fused_computation.62 | convolution fusion | flops 2150105088 | bytes 12582912 | tf_op jit(solution)/shard_map/dot_general | solution.py:58
  89.2 102.4 %reduce-scatter.3.cloned.1.call-done = f32[128,1024]{0,1:T(8,128)} async-done(((f32[2048,1024]{0,1:T(8,128)}), f32[128,1024]{0,1:T(8,128)}) %reduce-scatter.3.cloned.1.call-update) | async-done | bytes 524304 | tf_op jit(solution)/shard_map/reduce_scatter | solution.py:57
  191.5 2.6 fusion.22
  194.2 91.7 %all-reduce.101.cloned.1.call-done = f32[1024,150]{0,1:T(8,128)} async-done(((f32[1024,150]{0,1:T(8,128)}), f32[1024,150]{0,1:T(8,128)}) %all-reduce.101.cloned.1.call-update) | async-done | bytes 614416 | tf_op jit(solution)/shard_map/psum | solution.py:67
  285.9 1.1 reduce_max.9
  287.0 1.2 select_reduce_fusion
  288.2 1.7 fusion.23
  290.9 2.5 multiply_reduce_fusion.1
  293.7 53.5 %all-gather.5.cloned.1.call-done = bf16[2048,1024]{0,1:T(8,128)(2,1)} async-done(((bf16[128,1024]{0,1:T(8,128)(2,1)}), bf16[2048,1024]{0,1:T(8,128)(2,1)}) %all-gather.5.cloned.1.call-update) | async-done | bytes 4194320 | tf_op jit(solution)/shard_map/all_gather | solution.py:82
  347.2 6.5 %fusion.15 = bf16[512,1024]{0,1:T(8,128)(2,1)S(1)} fusion(f32[1024,512]{1,0:T(8,128)} %copy-done.7, bf16[2048,1024]{0,1:T(8,128)(2,1)} %all-gather.5.cloned.1.call-done, bf16[512,2048]{1,0:T(8,128)(2,1)} %param.13), kind=kOutput, calls=%fused_computation.69 | convolution fusion | flops 2152726528 | bytes 9437184 | tf_op jit(solution)/shard_map/dot_general | solution.py:84
  353.7 3.0 fusion.6
  357.3 5.4 %fusion.8 = f32[2048,1024]{0,1:T(8,128)} fusion(bf16[2048,1024]{0,1:T(8,128)(2,1)S(1)} %copy-done.3, f32[1024,2048]{1,0:T(8,128)S(1)} %get-tuple-element.158, f32[1024]{0:T(1024)S(1)} %get-tuple-element.159, f32[1024]{0:T(1024)S(1)} %get-tuple-element.160, f32[2048]{0:T(1024)S(1)} %copy-done.13, f32[1024]{0:T(1024)S(1)} %add_rsqrt_fusion, ...), kind=kLoop, calls=%fused_computation.10 | loop fusion | flops 16777216 | bytes 20996096 | tf_op jit(solution)/shard_map/mul | solution.py:96
  364.1 1.5 fusion.21
  365.6 7.4 %fusion.32 = f32[512,2048]{1,0:T(8,128)} fusion(bf16[512,1024]{0,1:T(8,128)(2,1)} %copy-done.10, bf16[2048,1024]{0,1:T(8,128)(2,1)} %copy-done.4), kind=kOutput, calls=%fused_computation.255 | convolution fusion | flops 2147483648 | bytes 9437184 | tf_op jit(solution)/shard_map/dot_general | solution.py:89
  372.9 4.5 fusion.28
  377.5 88.5 %reduce-scatter.5.cloned.1.call-done = f32[128,1024]{0,1:T(8,128)} async-done(((f32[2048,1024]{0,1:T(8,128)}), f32[128,1024]{0,1:T(8,128)}) %reduce-scatter.5.cloned.1.call-update) | async-done | bytes 524304 | tf_op jit(solution)/shard_map/reduce_scatter | solution.py:101
  465.9 2.9 broadcast_multiply_fusion.2
  470.0 2.4 broadcast_multiply_fusion
  472.4 6.0 %pad_add_fusion = f32[128,38,38]{0,2,1:T(8,128)S(1)} fusion(f32[128,32,32]{0,2,1:T(8,128)S(1)} %get-tuple-element.66, f32[128,32,32]{0,2,1:T(8,128)S(1)} %get-tuple-element.67, f32[128,32,32]{0,2,1:T(8,128)S(1)} %get-tuple-element.68, f32[128,32,32]{0,2,1:T(8,128)S(1)} %get-tuple-element.69, f32[128,32,32]{0,2,1:T(8,128)S(1)} %get-tuple-element.70, ...), kind=kLoop, calls=%fused_computation.76 | loop fusion | flops 7762944 | bytes 23283712 | tf_op jit(solution)/shard_map/transpose(jvp())/add_any | solution.py:22
  478.4 3.1 pad_add_fusion.1
  481.5 2.1 copy.21
  483.5 2.1 add.438
  486.4 1.4 multiply_reduce_fusion.49
  487.8 1.4 multiply_reduce_fusion.50
  (116 shorter events, 9.8 us)
Async XLA Ops:
  7.2 71.8 %copy-start = (bf16[512,2048]{1,0:T(8,128)(2,1)S(1)}, bf16[512,2048]{1,0:T(8,128)(2,1)}, u32[]{:S(2)}) copy-start(bf16[512,2048]{1,0:T(8,128)(2,1)} %param.12) | copy-start | bytes 6291460
  7.2 65.3 %all-gather.3.cloned.1.call-start = ((), (), s32[]{:S(2)}) async-start(), calls=%async_computation.2 | async-start | bytes 4456448 | tf_op jit(solution)/shard_map/all_gather | solution.py:42
  9.2 67.9 %copy-start.29 = (f32[128]{0:T(128)}, f32[128]{0:T(128)S(1)}, u32[]{:S(2)}) copy-start(f32[128]{0:T(128)S(1)} %get-tuple-element.110) | copy-start | bytes 1540
  9.2 67.9 %copy-start.30 = (f32[128]{0:T(128)}, f32[128]{0:T(128)S(1)}, u32[]{:S(2)}) copy-start(f32[128]{0:T(128)S(1)} %get-tuple-element.111) | copy-start | bytes 1540
  9.2 67.9 %copy-start.31 = (f32[128]{0:T(128)}, f32[128]{0:T(128)S(1)}, u32[]{:S(2)}) copy-start(f32[128]{0:T(128)S(1)} %get-tuple-element.112) | copy-start | bytes 1540
  9.2 67.9 %copy-start.32 = (f32[128]{0:T(128)}, f32[128]{0:T(128)S(1)}, u32[]{:S(2)}) copy-start(f32[128]{0:T(128)S(1)} %get-tuple-element.113) | copy-start | bytes 1540
  9.3 67.9 %copy-start.33 = (f32[128]{0:T(128)}, f32[128]{0:T(128)S(1)}, u32[]{:S(2)}) copy-start(f32[128]{0:T(128)S(1)} %get-tuple-element.114) | copy-start | bytes 1540
  9.3 67.9 %copy-start.34 = (f32[128]{0:T(128)}, f32[128]{0:T(128)S(1)}, u32[]{:S(2)}) copy-start(f32[128]{0:T(128)S(1)} %get-tuple-element.115) | copy-start | bytes 1540
  9.3 67.9 %copy-start.35 = (f32[128]{0:T(128)}, f32[128]{0:T(128)S(1)}, u32[]{:S(2)}) copy-start(f32[128]{0:T(128)S(1)} %get-tuple-element.116) | copy-start | bytes 1540
  9.3 67.9 %copy-start.36 = (f32[128]{0:T(128)}, f32[128]{0:T(128)S(1)}, u32[]{:S(2)}) copy-start(f32[128]{0:T(128)S(1)} %get-tuple-element.117) | copy-start | bytes 1540
  9.3 67.9 %copy-start.37 = (f32[128]{0:T(128)}, f32[128]{0:T(128)S(1)}, u32[]{:S(2)}) copy-start(f32[128]{0:T(128)S(1)} %get-tuple-element.118) | copy-start | bytes 1540
  9.3 67.9 %copy-start.38 = (f32[128]{0:T(128)}, f32[128]{0:T(128)S(1)}, u32[]{:S(2)}) copy-start(f32[128]{0:T(128)S(1)} %get-tuple-element.119) | copy-start | bytes 1540
  9.3 67.9 %copy-start.39 = (f32[128]{0:T(128)}, f32[128]{0:T(128)S(1)}, u32[]{:S(2)}) copy-start(f32[128]{0:T(128)S(1)} %get-tuple-element.120) | copy-start | bytes 1540
  9.3 67.9 %copy-start.40 = (f32[128]{0:T(128)}, f32[128]{0:T(128)S(1)}, u32[]{:S(2)}) copy-start(f32[128]{0:T(128)S(1)} %get-tuple-element.121) | copy-start | bytes 1540
  10.4 65.1 %copy-start.20 = (f32[128]{0:T(128)}, f32[128]{0:T(128)S(1)}, u32[]{:S(2)}) copy-start(f32[128]{0:T(128)S(1)} %get-tuple-element.136) | copy-start | bytes 1540
  10.4 65.1 %copy-start.22 = (f32[128]{0:T(128)}, f32[128]{0:T(128)S(1)}, u32[]{:S(2)}) copy-start(f32[128]{0:T(128)S(1)} %get-tuple-element.137) | copy-start | bytes 1540
  10.4 66.9 %copy-start.24 = (f32[128]{0:T(128)}, f32[128]{0:T(128)S(1)}, u32[]{:S(2)}) copy-start(f32[128]{0:T(128)S(1)} %get-tuple-element.138) | copy-start | bytes 1540
  10.4 66.9 %copy-start.26 = (f32[128]{0:T(128)}, f32[128]{0:T(128)S(1)}, u32[]{:S(2)}) copy-start(f32[128]{0:T(128)S(1)} %get-tuple-element.139) | copy-start | bytes 1540
  16.4 175.1 %reduce-scatter.3.cloned.1.call-start = ((), (), s32[]{:S(2)}) async-start(), calls=%async_computation.3 | async-start | bytes 8912896 | tf_op jit(solution)/shard_map/reduce_scatter | solution.py:57
  88.3 198.7 %copy-start.41 = (s32[1024]{0:T(1024)S(1)}, s32[1024]{0:T(1024)}, u32[]{:S(2)}) copy-start(s32[1024]{0:T(1024)} %param.15) | copy-start | bytes 12292
  88.4 197.5 %all-reduce.101.cloned.1.call-start = ((), (), s32[]{:S(2)}) async-start(), calls=%async_computation.4 | async-start | bytes 1245184 | tf_op jit(solution)/shard_map/psum | solution.py:67
  89.2 105.0 %copy-start.43 = (f32[128]{0:T(128)}, f32[128]{0:T(128)S(1)}, u32[]{:S(2)}) copy-start(f32[128]{0:T(128)S(1)} %dynamic_slice.7) | copy-start | bytes 1540
  194.1 153.1 %all-gather.5.cloned.1.call-start = ((), (), s32[]{:S(2)}) async-start(), calls=%async_computation.5 | async-start | bytes 4456448 | tf_op jit(solution)/shard_map/all_gather | solution.py:82
  289.9 63.7 %copy-start.11 = (f32[128,1024]{1,0:T(8,128)}, f32[128,1024]{1,0:T(8,128)S(1)}, u32[]{:S(2)}) copy-start(f32[128,1024]{1,0:T(8,128)S(1)} %fusion.23) | copy-start | bytes 1572868
  293.4 172.5 %reduce-scatter.5.cloned.1.call-start = ((), (), s32[]{:S(2)}) async-start(), calls=%async_computation.6 | async-start | bytes 8912896 | tf_op jit(solution)/shard_map/reduce_scatter | solution.py:101
  377.4 91.4 %copy-start.15 = (f32[128]{0:T(128)S(1)}, f32[128]{0:T(128)}, u32[]{:S(2)}) copy-start(f32[128]{0:T(128)} %copy-done.14) | copy-start | bytes 1540
  377.4 91.4 %copy-start.17 = (f32[128]{0:T(128)S(1)}, f32[128]{0:T(128)}, u32[]{:S(2)}) copy-start(f32[128]{0:T(128)} %copy-done.16) | copy-start | bytes 1540
  377.4 91.4 %copy-start.19 = (f32[128]{0:T(128)S(1)}, f32[128]{0:T(128)}, u32[]{:S(2)}) copy-start(f32[128]{0:T(128)} %copy-done.18) | copy-start | bytes 1540
  377.5 91.4 %copy-start.21 = (f32[128]{0:T(128)S(1)}, f32[128]{0:T(128)}, u32[]{:S(2)}) copy-start(f32[128]{0:T(128)} %copy-done.20) | copy-start | bytes 1540
  377.5 91.4 %copy-start.23 = (f32[128]{0:T(128)S(1)}, f32[128]{0:T(128)}, u32[]{:S(2)}) copy-start(f32[128]{0:T(128)} %copy-done.22) | copy-start | bytes 1540
  377.5 91.4 %copy-start.25 = (f32[128]{0:T(128)S(1)}, f32[128]{0:T(128)}, u32[]{:S(2)}) copy-start(f32[128]{0:T(128)} %copy-done.24) | copy-start | bytes 1540
  377.5 91.4 %copy-start.27 = (f32[128]{0:T(128)S(1)}, f32[128]{0:T(128)}, u32[]{:S(2)}) copy-start(f32[128]{0:T(128)} %copy-done.26) | copy-start | bytes 1540
  (19 other events, 197.3 us)
Sparse Core Ops, SparseCore 0:
  16.5 55.9 all-gather.2
  88.5 103.0 reduce-scatter.2
  195.5 90.2 all-reduce.100
  293.5 53.5 all-gather.4
  362.9 102.9 reduce-scatter.4
where the time goes:
time: 498 us
  waiting for transfers between devices  392 us (79%)
  other arithmetic  44 us (9%)
  matrix products  35 us (7%)
  between operations  16.2 us (3%)
  local copies, waits for them, and re-layouts  9.9 us (2%)
    reduce_scatter x1, waiting for transfers between devices, per_device(): lax.psum_scatter(lax.dot_general(w_cols, hidden, (((0,), (0,)), ((), ()))...  102 us
    psum x1, waiting for transfers between devices, per_device(): logits = lax.psum(part_logits, 'ch')  91.7 us
    reduce_scatter x1, waiting for transfers between devices, per_device(): lax.psum_scatter(conv_term, 'ch', scatter_dimension=0, tiled=True)  88.5 us
    all_gather x1, waiting for transfers between devices, per_device(): conv_all = lax.all_gather(conv_out, 'ch', axis=0, tiled=True)  56 us
    all_gather x1, waiting for transfers between devices, per_device(): incoming = lax.all_gather(branch_grad, 'ch', axis=0, tiled=True)  53.5 us
  transfers between devices with their start and end apart: 5, of which 5 were waited for; matrix products, arithmetic and copies ran while one was open for 3% of the time, Pallas kernels for 0%

commit v1 on v0

--- a/solution.py
+++ b/solution.py
@@ -64,7 +64,7 @@
     )
     block_out = inputs_wide + my_scale[:, None] * branch_sum
     part_logits = lax.dot_general(block_out, my_head, (((0,), (0,)), ((), ())), precision=highest)
-    logits = lax.psum(part_logits, "ch")
+    logits = jnp.sum(lax.all_gather(part_logits, "ch"), axis=0)
     row_max = jnp.max(logits, axis=1, keepdims=True)
     exp_terms = jnp.exp(logits - row_max)
     exp_total = jnp.sum(exp_terms, axis=1, keepdims=True)

time: 498 us -> 513 us (1.030); the launches traced: 498 us -> 505 us
  local copies, waits for them, and re-layouts: 9.9 us -> 23.6 us
  waiting for transfers between devices: 392 us -> 382 us
    psum x1 -> x0, waiting for transfers between devices: 91.7 us -> none  [per_device(): logits = lax.psum(part_logits, 'ch')]
    all_gather x0 -> x1, waiting for transfers between devices: none -> 84.4 us  [per_device(): logits = jnp.sum(lax.all_gather(part_logits, 'ch'), axis=0)]
    unnamed x93 -> x190, local copies, waits for them, and re-layouts: 3.12 us -> 15.2 us
where the time goes in v1:
time: 513 us; the launch traced here: 505 us
  waiting for transfers between devices  382 us (74%)
  other arithmetic  45.6 us (9%)
  matrix products  35.5 us (7%)
  local copies, waits for them, and re-layouts  23.6 us (5%)
  between operations  17.4 us (3%)
    reduce_scatter x1, waiting for transfers between devices, per_device(): lax.psum_scatter(lax.dot_general(w_cols, hidden, (((0,), (0,)), ((), ()))...  102 us
    reduce_scatter x1, waiting for transfers between devices, per_device(): lax.psum_scatter(conv_term, 'ch', scatter_dimension=0, tiled=True)  88.3 us
    all_gather x1, waiting for transfers between devices, per_device(): logits = jnp.sum(lax.all_gather(part_logits, 'ch'), axis=0)  84.4 us
    all_gather x1, waiting for transfers between devices, per_device(): conv_all = lax.all_gather(conv_out, 'ch', axis=0, tiled=True)  56 us
    all_gather x1, waiting for transfers between devices, per_device(): incoming = lax.all_gather(branch_grad, 'ch', axis=0, tiled=True)  51.3 us
    unnamed x190, local copies, waits for them, and re-layouts  15.2 us
  transfers between devices with their start and end apart: 5, of which 5 were waited for; matrix products, arithmetic and copies ran while one was open for 3% of the time, Pallas kernels for 0%

profile of v1, /device:TPU:0, one launch (start us, length us, event | category | flops | bytes accessed | tf_op | source)
XLA Modules:
  0.0 505.1 jit_solution(2474564495130163656)
XLA Ops:
  8.3 1.6 slice_bitcast_fusion.48
  12.4 5.4 %add_convert_fusion = bf16[128,32,32]{0,2,1:T(8,128)(2,1)} fusion(f32[128,32,32]{0,2,1:T(8,128)S(1)} %bitcast_convert_fusion, f32[128]{0:T(128)S(1)} %get-tuple-element.155, f32[128]{0:T(128)S(1)} %get-tuple-element.156, f32[128]{0:T(128)S(1)} %get-tuple-element.109, f32[128]{0:T(128)S(1)} %get-tuple-element.110, f32[128]{0:T(128)S(1)} %get-tuple-element.111, ...), kind=kLoop, calls=%fused_computation.141 | loop fusion | flops 12845056 | bytes 811520 | tf_op jit(solution)/shard_map/convert_element_type | solution.py:41
  17.8 56.0 %all-gather.5.cloned.1.call-done = bf16[2048,1024]{0,1:T(8,128)(2,1)} async-done(((bf16[128,1024]{0,1:T(8,128)(2,1)}), bf16[2048,1024]{0,1:T(8,128)(2,1)}) %all-gather.5.cloned.1.call-update) | async-done | bytes 4194320 | tf_op jit(solution)/shard_map/all_gather | solution.py:42
  73.8 3.0 convert_reduce_fusion
  78.9 1.6 fusion.5
  80.6 2.4 fusion.31
  83.0 1.3 copy-done.7
  84.3 5.6 %convolution_bitcast_fusion = f32[2048,1024]{0,1:T(8,128)} fusion(bf16[512,2048]{1,0:T(8,128)(2,1)S(1)} %copy-done.93, f32[1024,512]{1,0:T(8,128)S(1)} %fusion.31), kind=kOutput, calls=%fused_computation.63 | convolution fusion | flops 2150105088 | bytes 12582912 | tf_op jit(solution)/shard_map/dot_general | solution.py:58
  90.7 102.3 %reduce-scatter.3.cloned.1.call-done = f32[128,1024]{0,1:T(8,128)} async-done(((f32[2048,1024]{0,1:T(8,128)}), f32[128,1024]{0,1:T(8,128)}) %reduce-scatter.3.cloned.1.call-update) | async-done | bytes 524304 | tf_op jit(solution)/shard_map/reduce_scatter | solution.py:57
  193.1 2.6 fusion.22
  195.9 84.4 %all-gather.9.cloned.1.call-done = f32[16384,150]{0,1:T(8,128)} async-done(((f32[1024,150]{0,1:T(8,128)}), f32[16384,150]{0,1:T(8,128)}) %all-gather.9.cloned.1.call-update) | async-done | bytes 9830416 | tf_op jit(solution)/shard_map/all_gather | solution.py:67
  280.3 11.9 %copy.27 = f32[19,8,16,1024]{3,2,1,0:T(8,128)S(1)} copy(f32[19,8,16,1024]{3,1,2,0:T(8,128)} %bitcast.249) | data formatting | bytes 19922944
  292.2 2.3 bitcast_reduce_fusion
  295.4 2.2 fusion.23
  297.6 2.0 copy.24
  299.7 2.5 multiply_reduce_fusion.1
  302.4 51.3 %all-gather.7.cloned.1.call-done = bf16[2048,1024]{0,1:T(8,128)(2,1)} async-done(((bf16[128,1024]{0,1:T(8,128)(2,1)}), bf16[2048,1024]{0,1:T(8,128)(2,1)}) %all-gather.7.cloned.1.call-update) | async-done | bytes 4194320 | tf_op jit(solution)/shard_map/all_gather | solution.py:82
  353.7 6.5 %fusion.15 = bf16[512,1024]{0,1:T(8,128)(2,1)S(1)} fusion(f32[1024,512]{1,0:T(8,128)} %copy-done.7, bf16[2048,1024]{0,1:T(8,128)(2,1)} %all-gather.7.cloned.1.call-done, bf16[512,2048]{1,0:T(8,128)(2,1)} %param.13), kind=kOutput, calls=%fused_computation.70 | convolution fusion | flops 2152726528 | bytes 9437184 | tf_op jit(solution)/shard_map/dot_general | solution.py:84
  360.2 3.0 fusion.6
  363.9 5.4 %fusion.8 = f32[2048,1024]{0,1:T(8,128)} fusion(bf16[2048,1024]{0,1:T(8,128)(2,1)S(1)} %copy-done.3, f32[1024,2048]{1,0:T(8,128)S(1)} %get-tuple-element.158, f32[1024]{0:T(1024)S(1)} %get-tuple-element.159, f32[1024]{0:T(1024)S(1)} %get-tuple-element.160, f32[2048]{0:T(1024)S(1)} %copy-done.11, f32[1024]{0:T(1024)S(1)} %add_rsqrt_fusion, ...), kind=kLoop, calls=%fused_computation.11 | loop fusion | flops 16777216 | bytes 20996096 | tf_op jit(solution)/shard_map/mul | solution.py:96
  370.6 1.5 fusion.21
  372.0 7.4 %fusion.32 = f32[512,2048]{1,0:T(8,128)} fusion(bf16[512,1024]{0,1:T(8,128)(2,1)} %copy-done.9, bf16[2048,1024]{0,1:T(8,128)(2,1)} %copy-done.4), kind=kOutput, calls=%fused_computation.256 | convolution fusion | flops 2147483648 | bytes 9437184 | tf_op jit(solution)/shard_map/dot_general | solution.py:89
  379.5 4.5 fusion.28
  384.1 88.3 %reduce-scatter.5.cloned.1.call-done = f32[128,1024]{0,1:T(8,128)} async-done(((f32[2048,1024]{0,1:T(8,128)}), f32[128,1024]{0,1:T(8,128)}) %reduce-scatter.5.cloned.1.call-update) | async-done | bytes 524304 | tf_op jit(solution)/shard_map/reduce_scatter | solution.py:101
  472.5 3.0 broadcast_multiply_fusion.2
  477.0 2.4 broadcast_multiply_fusion
  479.4 6.1 %pad_add_fusion = f32[128,38,38]{0,2,1:T(8,128)S(1)} fusion(f32[128,32,32]{0,2,1:T(8,128)S(1)} %get-tuple-element.66, f32[128,32,32]{0,2,1:T(8,128)S(1)} %get-tuple-element.67, f32[128,32,32]{0,2,1:T(8,128)S(1)} %get-tuple-element.68, f32[128,32,32]{0,2,1:T(8,128)S(1)} %get-tuple-element.69, f32[128,32,32]{0,2,1:T(8,128)S(1)} %get-tuple-element.70, ...), kind=kLoop, calls=%fused_computation.77 | loop fusion | flops 7762944 | bytes 23283712 | tf_op jit(solution)/shard_map/transpose(jvp())/add_any | solution.py:22
  485.5 3.1 pad_add_fusion.1
  488.5 2.0 copy.25
  490.6 2.1 add.436
  493.4 1.4 multiply_reduce_fusion.49
  494.8 1.4 multiply_reduce_fusion.50
  (214 shorter events, 11.4 us)
Async XLA Ops:
  7.2 66.7 %all-gather.5.cloned.1.call-start = ((), (), s32[]{:S(2)}) async-start(), calls=%async_computation.2 | async-start | bytes 4456448 | tf_op jit(solution)/shard_map/all_gather | solution.py:42
  17.8 175.3 %reduce-scatter.3.cloned.1.call-start = ((), (), s32[]{:S(2)}) async-start(), calls=%async_computation.3 | async-start | bytes 8912896 | tf_op jit(solution)/shard_map/reduce_scatter | solution.py:57
  89.9 190.4 %all-gather.9.cloned.1.call-start = ((), (), s32[]{:S(2)}) async-start(), calls=%async_computation.6 | async-start | bytes 10584064 | tf_op jit(solution)/shard_map/all_gather | solution.py:67
  90.7 201.5 %copy-start.91 = (f32[128]{0:T(128)}, f32[128]{0:T(128)S(1)}, u32[]{:S(2)}) copy-start(f32[128]{0:T(128)S(1)} %dynamic_slice.7) | copy-start | bytes 1540
  195.6 158.1 %all-gather.7.cloned.1.call-start = ((), (), s32[]{:S(2)}) async-start(), calls=%async_computation.4 | async-start | bytes 4456448 | tf_op jit(solution)/shard_map/all_gather | solution.py:82
  302.2 170.2 %reduce-scatter.5.cloned.1.call-start = ((), (), s32[]{:S(2)}) async-start(), calls=%async_computation.5 | async-start | bytes 8912896 | tf_op jit(solution)/shard_map/reduce_scatter | solution.py:101
  379.4 93.0 %copy-start.75 = (f32[128]{0:T(128)S(1)}, f32[128]{0:T(128)}, u32[]{:S(2)}) copy-start(f32[128]{0:T(128)} %copy-done.74) | copy-start | bytes 1540
  379.4 93.0 %copy-start.77 = (f32[128]{0:T(128)S(1)}, f32[128]{0:T(128)}, u32[]{:S(2)}) copy-start(f32[128]{0:T(128)} %copy-done.76) | copy-start | bytes 1540
  379.4 93.0 %copy-start.79 = (f32[128]{0:T(128)S(1)}, f32[128]{0:T(128)}, u32[]{:S(2)}) copy-start(f32[128]{0:T(128)} %copy-done.78) | copy-start | bytes 1540
  379.4 93.0 %copy-start.81 = (f32[128]{0:T(128)S(1)}, f32[128]{0:T(128)}, u32[]{:S(2)}) copy-start(f32[128]{0:T(128)} %copy-done.80) | copy-start | bytes 1540
  379.4 93.0 %copy-start.83 = (f32[128]{0:T(128)S(1)}, f32[128]{0:T(128)}, u32[]{:S(2)}) copy-start(f32[128]{0:T(128)} %copy-done.82) | copy-start | bytes 1540
  379.4 93.0 %copy-start.85 = (f32[128]{0:T(128)S(1)}, f32[128]{0:T(128)}, u32[]{:S(2)}) copy-start(f32[128]{0:T(128)} %copy-done.84) | copy-start | bytes 1540
  379.5 93.0 %copy-start.87 = (f32[128]{0:T(128)S(1)}, f32[128]{0:T(128)}, u32[]{:S(2)}) copy-start(f32[128]{0:T(128)} %copy-done.86) | copy-start | bytes 1540
  379.5 93.0 %copy-start.89 = (f32[128]{0:T(128)S(1)}, f32[128]{0:T(128)}, u32[]{:S(2)}) copy-start(f32[128]{0:T(128)} %copy-done.88) | copy-start | bytes 1540
  384.0 91.5 %copy-start.39 = (f32[128]{0:T(128)S(1)}, f32[128]{0:T(128)}, u32[]{:S(2)}) copy-start(f32[128]{0:T(128)} %copy-done.38) | copy-start | bytes 1540
  384.0 91.5 %copy-start.41 = (f32[128]{0:T(128)S(1)}, f32[128]{0:T(128)}, u32[]{:S(2)}) copy-start(f32[128]{0:T(128)} %copy-done.40) | copy-start | bytes 1540
  384.0 91.5 %copy-start.43 = (f32[128]{0:T(128)S(1)}, f32[128]{0:T(128)}, u32[]{:S(2)}) copy-start(f32[128]{0:T(128)} %copy-done.42) | copy-start | bytes 1540
  384.0 91.5 %copy-start.45 = (f32[128]{0:T(128)S(1)}, f32[128]{0:T(128)}, u32[]{:S(2)}) copy-start(f32[128]{0:T(128)} %copy-done.44) | copy-start | bytes 1540
  384.0 91.5 %copy-start.47 = (f32[128]{0:T(128)S(1)}, f32[128]{0:T(128)}, u32[]{:S(2)}) copy-start(f32[128]{0:T(128)} %copy-done.46) | copy-start | bytes 1540
  384.0 91.5 %copy-start.49 = (f32[128]{0:T(128)S(1)}, f32[128]{0:T(128)}, u32[]{:S(2)}) copy-start(f32[128]{0:T(128)} %copy-done.48) | copy-start | bytes 1540
  384.0 91.5 %copy-start.51 = (f32[128]{0:T(128)S(1)}, f32[128]{0:T(128)}, u32[]{:S(2)}) copy-start(f32[128]{0:T(128)} %copy-done.50) | copy-start | bytes 1540
  384.0 91.5 %copy-start.53 = (f32[128]{0:T(128)S(1)}, f32[128]{0:T(128)}, u32[]{:S(2)}) copy-start(f32[128]{0:T(128)} %copy-done.52) | copy-start | bytes 1540
  384.0 91.5 %copy-start.55 = (f32[128]{0:T(128)S(1)}, f32[128]{0:T(128)}, u32[]{:S(2)}) copy-start(f32[128]{0:T(128)} %copy-done.54) | copy-start | bytes 1540
  384.0 91.5 %copy-start.57 = (f32[128]{0:T(128)S(1)}, f32[128]{0:T(128)}, u32[]{:S(2)}) copy-start(f32[128]{0:T(128)} %copy-done.56) | copy-start | bytes 1540
  384.1 91.5 %copy-start.59 = (f32[128]{0:T(128)S(1)}, f32[128]{0:T(128)}, u32[]{:S(2)}) copy-start(f32[128]{0:T(128)} %copy-done.58) | copy-start | bytes 1540
  384.1 91.5 %copy-start.61 = (f32[128]{0:T(128)S(1)}, f32[128]{0:T(128)}, u32[]{:S(2)}) copy-start(f32[128]{0:T(128)} %copy-done.60) | copy-start | bytes 1540
  384.1 91.5 %copy-start.63 = (f32[128]{0:T(128)S(1)}, f32[128]{0:T(128)}, u32[]{:S(2)}) copy-start(f32[128]{0:T(128)} %copy-done.62) | copy-start | bytes 1540
  384.1 91.5 %copy-start.65 = (f32[128]{0:T(128)S(1)}, f32[128]{0:T(128)}, u32[]{:S(2)}) copy-start(f32[128]{0:T(128)} %copy-done.64) | copy-start | bytes 1540
  384.1 91.5 %copy-start.67 = (f32[128]{0:T(128)S(1)}, f32[128]{0:T(128)}, u32[]{:S(2)}) copy-start(f32[128]{0:T(128)} %copy-done.66) | copy-start | bytes 1540
  384.1 91.5 %copy-start.69 = (f32[128]{0:T(128)S(1)}, f32[128]{0:T(128)}, u32[]{:S(2)}) copy-start(f32[128]{0:T(128)} %copy-done.68) | copy-start | bytes 1540
  384.1 91.5 %copy-start.71 = (f32[128]{0:T(128)S(1)}, f32[128]{0:T(128)}, u32[]{:S(2)}) copy-start(f32[128]{0:T(128)} %copy-done.70) | copy-start | bytes 1540
  384.1 91.5 %copy-start.73 = (f32[128]{0:T(128)S(1)}, f32[128]{0:T(128)}, u32[]{:S(2)}) copy-start(f32[128]{0:T(128)} %copy-done.72) | copy-start | bytes 1540
  (67 other events, 2743.9 us)
Sparse Core Ops, SparseCore 0:
  17.9 55.9 all-gather.4
  90.0 103.0 reduce-scatter.2
  195.8 84.4 all-gather.8
  302.3 51.3 all-gather.6
  369.4 102.9 reduce-scatter.4
